TPU v7x, 32 devices: a whole 2x2x4 slice. The times are simulated.
32 devices in a mesh: groups: 2 (over x), sect: 2 (over core), tile: 8 (over z, y).
Axes of the slice: x: 2, y: 2, z: 4, core: 2. Of those that a mesh axis runs over, the one named last changes fastest.
Arguments:
- features: bfloat16 [4, 16, 64, 512], P(('groups', 'sect'), 'tile'), parts along dimension 0, may hold values from -6 to 6
- conv_first: bfloat16 [3, 3, 3, 512, 512], replicated, may hold values from -0.0546875 to 0.0546875
- bias_first: bfloat16 [512], replicated, may hold values from -3 to 3
- conv_second: bfloat16 [3, 3, 3, 512, 256], replicated, may hold values from -0.0546875 to 0.0546875
- bias_second: bfloat16 [256], replicated, may hold values from -3 to 3
- conv_third: bfloat16 [3, 3, 3, 256, 128], replicated, may hold values from -0.078125 to 0.078125
- bias_third: bfloat16 [128], replicated, may hold values from -3 to 3
Outputs:
- decoded: bfloat16 [4, 64, 256, 128], P(('groups', 'sect'), 'tile'), parts along dimension 0
There are 2 independent parts, one for each index of `groups`. A program takes and returns all parts, laid end to end along the dimension named above; an argument that names none is the same for every part. Nothing has to cross between parts.
All inputs are finite; a program needn't handle non-finite values.
Results may differ from a plain program's by a relative error of at most 0.014.
Values may be sent and summed in bfloat16 or wider, within the bound.
A program may use at most 128 MiB of HBM per device.

v0:
```python
import functools

import jax
import jax.numpy as jnp
from jax import lax
from jax.experimental import pallas as pl
from jax.experimental.pallas import tpu as pltpu
from jax.sharding import PartitionSpec as P

MESH = pl.DeviceIdType.MESH
F32 = jnp.float32
BF16 = jnp.bfloat16


def silu(v):
    return v / (1.0 + jnp.exp(-v))


def merge_upsampled(read, write):
    taps = [[read(i, j) for j in range(3)] for i in range(3)]
    for p in range(2):
        for q in range(2):
            if p == 0:
                row = taps[0] if q == 0 else [taps[1][j] + taps[2][j] for j in range(3)]
            else:
                row = [taps[0][j] + taps[1][j] for j in range(3)] if q == 0 else taps[2]
            write(p, q, 0, 0, row[1] + row[2])
            write(p, q, 0, 1, row[0] + row[1])
            write(p, q, 1, 0, row[0])
            write(p, q, 1, 1, row[2])


def kernel(
    count, feat, w1h, b1, w2h, b2, w3h, b3, out,
    fbuf, sbuf, w1, w2, w3, m2, m3, mid, low, acc2, acc3, stage, obuf,
    w_sem, own_sem, out_sem, nb_send, nb_recv, fw_send, fw_recv, mid_send, mid_recv, low_send, low_recv,
):
    s = lax.axis_index("sect")
    t = lax.axis_index("tile")
    rows, cols, c1 = feat.shape[1], feat.shape[2], feat.shape[3]
    c2, c3 = w2h.shape[4], w3h.shape[4]
    h1, h2 = c1 // 2, c2 // 2
    total = rows + 4
    has_up, has_down = t > 0, t < count - 1
    up, down = lax.rem(t + count - 1, count), lax.rem(t + 1, count)
    sib = {"sect": 1 - s}

    own = pltpu.make_async_copy(feat.at[0], fbuf.at[s, pl.ds(2, rows)], own_sem)
    own.start()
    o1 = pl.multiple_of(s * h1, h1)
    o2 = pl.multiple_of(s * h2, h2)
    halves1 = [o1, pl.multiple_of((1 - s) * h1, h1)]
    halves2 = [o2, pl.multiple_of((1 - s) * h2, h2)]
    load1 = [
        pltpu.make_async_copy(w1h.at[:, :, j, :, pl.ds(o1, h1)], w1.at[:, :, j], w_sem.at[j])
        for j in range(3)
    ]
    load2 = [
        pltpu.make_async_copy(
            w2h.at[:, :, :, pl.ds(halves1[k], h1), pl.ds(o2, h2)], w2.at[k], w_sem.at[3 + k]
        )
        for k in range(2)
    ]
    load3 = [
        pltpu.make_async_copy(w3h.at[:, :, :, pl.ds(halves2[k], h2), :], w3.at[k], w_sem.at[5 + k])
        for k in range(2)
    ]
    for load in load1 + load2 + load3:
        load.start()

    barrier = pltpu.get_barrier_semaphore()
    pl.semaphore_signal(barrier, inc=1, device_id=sib, device_id_type=MESH)

    @pl.when(has_up)
    def _():
        pl.semaphore_signal(barrier, inc=1, device_id={"tile": up}, device_id_type=MESH)

    @pl.when(has_down)
    def _():
        pl.semaphore_signal(barrier, inc=1, device_id={"tile": down}, device_id_type=MESH)

    pl.semaphore_wait(barrier, 1 + has_up.astype(jnp.int32) + has_down.astype(jnp.int32))

    def remote(src, dst, send, recv, device):
        return pltpu.make_async_remote_copy(
            src_ref=src, dst_ref=dst, send_sem=send, recv_sem=recv, device_id=device, device_id_type=MESH
        )

    plan = [
        (rows - 1, 1, down, has_down, has_up),
        (0, rows + 2, up, has_up, has_down),
        (rows - 2, 0, down, has_down, has_up),
        (1, rows + 3, up, has_up, has_down),
    ]
    direct = [
        remote(feat.at[0, src], fbuf.at[s, dst], nb_send.at[n], nb_recv.at[n], {"tile": to})
        for n, (src, dst, to, _, _) in enumerate(plan)
    ]
    forward = [
        remote(fbuf.at[s, dst], fbuf.at[s, dst], fw_send.at[n], fw_recv.at[n], sib)
        for n, (_, dst, _, _, _) in enumerate(plan)
    ]
    swap = remote(feat.at[0], fbuf.at[s, pl.ds(2, rows)], fw_send.at[4], fw_recv.at[4], sib)
    for n in range(4):
        pl.when(plan[n][3])(direct[n].start)
    swap.start()

    def silu_rows(frame, row, size):
        sbuf[frame, pl.ds(row * cols, size * cols), :] = silu(
            fbuf[frame, pl.ds(row, size)].astype(F32)
        ).astype(BF16).reshape(size * cols, c1)

    for n in range(4):
        dst = plan[n][1]

        @pl.when(jnp.logical_not(plan[n][4]))
        def _(dst=dst):
            for f in range(2):
                fbuf[f, dst] = jnp.zeros((cols, c1), BF16)

    def early1(j):
        load1[j].wait()
        for i in range(3):
            w1[0, i, j] = w1[0, i, j] + w1[1, i, j]

    def pass_on(n):
        @pl.when(plan[n][4])
        def _():
            direct[n].wait_recv()
            forward[n].start()

    def arrived(n):
        @pl.when(plan[n][4])
        def _():
            forward[n].wait_recv()
        for f in range(2):
            silu_rows(f, plan[n][1], 1)

    early1(0)
    early1(1)
    early1(2)
    own.wait()
    swap.wait_recv()
    for f in range(2):
        silu_rows(f, 2, rows)
    pass_on(0)
    pass_on(1)

    def merge(buf, wide, half, c, size):
        def read(i, j):
            if c == 0:
                return buf[half, 0, i, j] + buf[half, 1, i, j]
            return buf[half, 2, i, j]

        def write(p, q, outer, phase, value):
            n = value.shape[1]
            wide[c, half, p, outer, pl.ds(q * size, size), pl.ds(phase * n, n)] = value

        merge_upsampled(read, write)

    for k in range(2):
        load2[k].wait()
        for c in range(2):
            merge(w2, m2, k, c, h1)
    for k in range(2):
        load3[k].wait()
        for c in range(2):
            merge(w3, m3, k, c, h2)

    def shifts(value):
        size = value.shape[0]
        place = lax.rem(lax.broadcasted_iota(jnp.int32, value.shape, 0), cols)

        def later():
            return jnp.where(place == 0, 0.0, pltpu.roll(value, 1, 0))

        def sooner():
            return jnp.where(place == cols - 1, 0.0, pltpu.roll(value, size - 1, 0))

        return later, sooner

    bias1 = b1[:, pl.ds(o1, h1)].astype(F32)
    bias2 = b2[:, pl.ds(o2, h2)].astype(F32)
    bias3 = b3[...].astype(F32)

    def first(hidden_rows):
        def gather(frames):
            return jnp.concatenate(
                [
                    jnp.concatenate(
                        [
                            sbuf[f, pl.ds((start + i) * cols, size * cols), :]
                            for i in range(3)
                        ],
                        axis=1,
                    )
                    for f in frames
                    for start, size in hidden_rows
                ],
                axis=0,
            )

        height = sum(size for _, size in hidden_rows) * cols
        both, earlier = gather((0, 1)), gather((0,))
        result = []
        summed = [None, None]
        for j in (1, 0, 2):
            kernel_now = w1[2, :, j].reshape(3 * c1, h1)
            kernel_early = w1[0, :, j].reshape(3 * c1, h1)
            now = jnp.dot(both, kernel_now, preferred_element_type=F32)
            early = jnp.dot(earlier, kernel_early, preferred_element_type=F32)
            for f in range(2):
                part = now[f * height : (f + 1) * height] + early
                if j == 1:
                    summed[f] = part
                else:
                    later, sooner = shifts(part)
                    summed[f] = summed[f] + (later() if j == 0 else sooner())
        for f in range(2):
            at = 0
            for start, size in hidden_rows:
                for row in range(start, start + size):
                    base = fbuf[f, row + 1, :, pl.ds(o1, h1)].astype(F32)
                    hidden = (base + (summed[f][at : at + cols] + bias1)).astype(BF16).astype(F32)
                    value = silu(hidden)
                    if row == 0:
                        value = jnp.where(has_up, value, 0.0)
                    if row == rows + 1:
                        value = jnp.where(has_down, value, 0.0)
                    mid[0, f, row] = value.astype(BF16)
                    at += cols

    arrived(0)
    arrived(1)
    first([(1, rows)])
    send_mid = [
        remote(mid.at[0, :, pl.ds(1, rows)], mid.at[1, :, pl.ds(1, rows)], mid_send.at[0], mid_recv.at[0], sib),
        remote(mid.at[0, :, 0], mid.at[1, :, 0], mid_send.at[1], mid_recv.at[1], sib),
        remote(mid.at[0, :, rows + 1], mid.at[1, :, rows + 1], mid_send.at[2], mid_recv.at[2], sib),
    ]
    send_mid[0].start()
    pass_on(2)
    pass_on(3)
    arrived(2)
    arrived(3)
    first([(0, 1), (rows + 1, 1)])
    send_mid[1].start()
    send_mid[2].start()

    lines = (rows + 1) * cols

    def second(half, then):
        def gather(f):
            return jnp.concatenate(
                [mid[half, f, pl.ds(q, rows + 1)].reshape(lines, h1) for q in range(2)], axis=1
            )

        earlier = gather(0)
        both = jnp.concatenate([earlier, gather(1)], axis=0)
        for p in range(2):
            for outer in range(2):
                now = jnp.dot(both, m2[1, half, p, outer], preferred_element_type=F32)
                early = jnp.dot(earlier, m2[0, half, p, outer], preferred_element_type=F32)
                for f in range(2):
                    then(p, outer, f, now[f * lines : (f + 1) * lines] + early)

    def keep(p, outer, f, value):
        acc2[p, outer, f] = value

    def add(p, outer, f, value):
        acc2[p, outer, f] = acc2[p, outer, f] + value

    second(0, keep)
    for copy in send_mid:
        copy.wait_recv()
    second(1, add)

    send_low = [
        remote(low.at[0, f], low.at[1, f], low_send.at[f], low_recv.at[f], sib) for f in range(2)
    ]
    last = 2 * rows + 1
    for f in range(2):
        for p in range(2):
            inner, outer = acc2[p, 0, f], acc2[p, 1, f]
            values = [
                inner[:, :h2] + shifts(outer[:, :h2])[0](),
                inner[:, h2:] + shifts(outer[:, h2:])[1](),
            ]
            for phase in range(2):
                value = silu(values[phase] + bias2)
                for m in range(rows + 1):
                    row = 2 * m + 1 - p
                    part = value[m * cols : (m + 1) * cols]
                    if row == 0:
                        part = jnp.where(has_up, part, 0.0)
                    if row == last:
                        part = jnp.where(has_down, part, 0.0)
                    low[0, f, phase, row] = part.astype(BF16)
        if f == 0:
            send_low[0].start()
        else:
            pl.when(s == 0)(send_low[1].start)

    deep = 2 * rows * cols

    def third(half, p, phase):
        x = jnp.concatenate(
            [
                low[half, f, phase, pl.ds(p + q, 2 * rows)].reshape(deep, h2)
                for f in (0, s)
                for q in range(2)
            ],
            axis=1,
        )
        return [
            jnp.dot(
                x,
                jnp.concatenate([m3[0, half, p, outer], m3[1, half, p, outer]], axis=0),
                preferred_element_type=F32,
            )
            for outer in range(2)
        ]

    for p in range(2):
        for phase in range(2):
            for outer, value in enumerate(third(0, p, phase)):
                acc3[p, phase, outer] = value
    send_low[0].wait_recv()
    pl.when(s == 1)(send_low[1].wait_recv)
    put = []
    for p in range(2):
        inner, outer = [], []
        for phase in range(2):
            a, b = third(1, p, phase)
            inner.append(acc3[p, phase, 0] + a)
            outer.append(acc3[p, phase, 1] + b)
        values = [
            inner[0][:, :c3] + shifts(outer[1][:, :c3])[0](),
            inner[0][:, c3:] + outer[1][:, c3:],
            inner[1][:, :c3] + outer[0][:, :c3],
            inner[1][:, c3:] + shifts(outer[0][:, c3:])[1](),
        ]
        for n in range(4):
            for m in range(2 * rows):
                stage[p, m, pl.ds(n, cols, stride=4), :] = values[n][m * cols : (m + 1) * cols] + bias3
        for m in range(2 * rows):
            row = 2 * m + p
            obuf[row] = stage[p, m].astype(BF16)
    copy = pltpu.make_async_copy(obuf, out.at[0], out_sem)
    copy.start()

    for n in range(4):
        pl.when(plan[n][3])(direct[n].wait_send)
        pl.when(plan[n][4])(forward[n].wait_send)
    swap.wait_send()
    for c in send_mid:
        c.wait_send()
    send_low[0].wait_send()
    pl.when(s == 0)(send_low[1].wait_send)
    copy.wait()


def per_device(features, w1, b1, w2, b2, w3, b3):
    count = lax.axis_size("tile")
    _, rows, cols, c1 = features.shape
    c2, c3 = w2.shape[4], w3.shape[4]
    h1, h2 = c1 // 2, c2 // 2
    anywhere = pl.BlockSpec(memory_space=pl.ANY)
    vmem = pl.BlockSpec(memory_space=pltpu.VMEM)
    dma = pltpu.SemaphoreType.DMA
    return pl.pallas_call(
        functools.partial(kernel, count),
        out_shape=jax.ShapeDtypeStruct((1, 4 * rows, 4 * cols, c3), BF16),
        in_specs=[anywhere, anywhere, vmem, anywhere, vmem, anywhere, vmem],
        out_specs=anywhere,
        scratch_shapes=[
            pltpu.VMEM((2, rows + 4, cols, c1), BF16),
            pltpu.VMEM((2, (rows + 4) * cols, c1), BF16),
            pltpu.VMEM((3, 3, 3, c1, h1), BF16),
            pltpu.VMEM((2, 3, 3, 3, h1, h2), BF16),
            pltpu.VMEM((2, 3, 3, 3, h2, c3), BF16),
            pltpu.VMEM((2, 2, 2, 2, 2 * h1, 2 * h2), BF16),
            pltpu.VMEM((2, 2, 2, 2, 2 * h2, 2 * c3), BF16),
            pltpu.VMEM((2, 2, rows + 2, cols, h1), BF16),
            pltpu.VMEM((2, 2, 2, 2 * rows + 2, cols, h2), BF16),
            pltpu.VMEM((2, 2, 2, (rows + 1) * cols, 2 * h2), F32),
            pltpu.VMEM((2, 2, 2, 2 * rows * cols, 2 * c3), F32),
            pltpu.VMEM((2, 2 * rows, 4 * cols, c3), F32),
            pltpu.VMEM((4 * rows, 4 * cols, c3), BF16),
            dma((7,)),
            dma(()),
            dma(()),
            dma((4,)),
            dma((4,)),
            dma((5,)),
            dma((5,)),
            dma((3,)),
            dma((3,)),
            dma((2,)),
            dma((2,)),
        ],
        compiler_params=pltpu.CompilerParams(
            collective_id=0, has_side_effects=True, vmem_limit_bytes=52 * 2**20
        ),
    )(features, w1, b1.reshape(1, c1), w2, b2.reshape(1, c2), w3, b3.reshape(1, c3))


def solution(mesh):
    return jax.shard_map(
        per_device,
        mesh=mesh,
        in_specs=(P(("groups", "sect"), "tile", None, None), P(), P(), P(), P(), P(), P()),
        out_specs=P(("groups", "sect"), "tile", None, None),
        check_vma=False,
    )
```

profile of v0, /device:TPU:9, one launch (start us, length us, event | category | flops | bytes accessed | tf_op | source)
XLA Modules:
  0.0 21.8 jit_solution(4341336394779851721)
XLA Ops:
  0.0 0.7 %reshape.10.b2 = bf16[1,256]{1,0:T(2,128)(2,1)S(1)} reshape(bf16[256]{0:T(256)(128)(2,1)} %param.11) | data formatting | bytes 1024 | tf_op jit(solution)/shard_map/reshape | solution.py:405
  0.7 0.7 %reshape.9.b1 = bf16[1,512]{1,0:T(2,128)(2,1)S(1)} reshape(bf16[512]{0:T(512)(128)(2,1)} %param.9) | data formatting | bytes 2048 | tf_op jit(solution)/shard_map/reshape | solution.py:405
  1.3 0.0 copy-start
  1.3 0.9 %copy-done = bf16[1,2,64,512]{3,2,1,0:T(8,128)(2,1)S(1)} copy-done((bf16[1,2,64,512]{3,2,1,0:T(8,128)(2,1)S(1)}, bf16[1,2,64,512]{3,2,1,0:T(8,128)(2,1)}, u32[]{:S(2)}) %copy-start) | copy-done | bytes 131096
  2.2 0.0 copy-start.1
  2.2 0.7 %copy-done.1 = bf16[128]{0:T(256)(128)(2,1)S(1)} copy-done((bf16[128]{0:T(256)(128)(2,1)S(1)}, bf16[128]{0:T(256)(128)(2,1)}, u32[]{:S(2)}) %copy-start.1) | copy-done | bytes 280
  2.9 18.0 %shard_map.73 = bf16[1,8,256,128]{3,2,1,0:T(8,128)(2,1)S(1)} custom-call(bf16[1,2,64,512]{3,2,1,0:T(8,128)(2,1)S(1)} %copy-done, bf16[3,3,3,512,512]{4,3,2,1,0:T(8,128)(2,1)} %w1h.1, bf16[1,512]{1,0:T(2,128)(2,1)S(1)} %reshape.9.b1, bf16[3,3,3,512,256]{4,3,2,1,0:T(8,128)(2,1)} %w2h.1, bf16[1,256]{1,0:T(2,128)(2,1)S(1)} %reshape.10.b2, ...), custom_call_target="tpu_custom_call" | custom-call | tf_op jit(solution)/shard_map/pallas_call | solution.py:371
  21.0 0.8 %copy.9 = bf16[1,8,256,128]{3,2,1,0:T(8,128)(2,1)} copy(bf16[1,8,256,128]{3,2,1,0:T(8,128)(2,1)S(1)} %shard_map.73) | data formatting | bytes 1048576
Async XLA Ops:
  1.3 0.9 %copy-start = (bf16[1,2,64,512]{3,2,1,0:T(8,128)(2,1)S(1)}, bf16[1,2,64,512]{3,2,1,0:T(8,128)(2,1)}, u32[]{:S(2)}) copy-start(bf16[1,2,64,512]{3,2,1,0:T(8,128)(2,1)} %feat.1) | copy-start | bytes 393220
  2.2 0.7 %copy-start.1 = (bf16[128]{0:T(256)(128)(2,1)S(1)}, bf16[128]{0:T(256)(128)(2,1)}, u32[]{:S(2)}) copy-start(bf16[128]{0:T(256)(128)(2,1)} %param.13) | copy-start | bytes 772
where the time goes:
time: 21.9 us; the launch traced here: 21.8 us
  Pallas kernels  18 us (82%)
  local copies, waits for them, and re-layouts  3.69 us (17%)
    pallas_call x1, Pallas kernels, per_device(): pl.pallas_call(functools.partial(kernel, count), out_shape=jax.ShapeDtype...  18 us
    unnamed x5, local copies, waits for them, and re-layouts  2.35 us
    reshape x1, local copies, waits for them, and re-layouts, per_device(): b1.reshape(1, c1)  0.68 us
    reshape x1, local copies, waits for them, and re-layouts, per_device(): b2.reshape(1, c2)  0.66 us

commit v1 on v0

--- a/solution.py
+++ b/solution.py
@@ -10,6 +10,7 @@
 MESH = pl.DeviceIdType.MESH
 F32 = jnp.float32
 BF16 = jnp.bfloat16
+PIECES = 2
 
 
 def silu(v):
@@ -31,18 +32,17 @@
 
 
 def kernel(
-    count, feat, w1h, b1, w2h, b2, w3h, b3, out,
-    fbuf, sbuf, w1, w2, w3, m2, m3, mid, low, acc2, acc3, stage, obuf,
-    w_sem, own_sem, out_sem, nb_send, nb_recv, fw_send, fw_recv, mid_send, mid_recv, low_send, low_recv,
+    count, feat, w1h, b1h, w2h, b2h, w3h, b3h, out,
+    fbuf, sbuf, b1, b2, b3, w1, w2, w3, m2, m3, mid, low, acc2, acc3, stage,
+    w_sem, own_sem, nb_send, nb_recv, fw_send, fw_recv, mid_send, mid_recv, low_send, low_recv,
 ):
     s = lax.axis_index("sect")
     t = lax.axis_index("tile")
     rows, cols, c1 = feat.shape[1], feat.shape[2], feat.shape[3]
     c2, c3 = w2h.shape[4], w3h.shape[4]
     h1, h2 = c1 // 2, c2 // 2
-    total = rows + 4
+    assert rows == 2 and count % 2 == 0
     has_up, has_down = t > 0, t < count - 1
-    up, down = lax.rem(t + count - 1, count), lax.rem(t + 1, count)
     sib = {"sect": 1 - s}
 
     own = pltpu.make_async_copy(feat.at[0], fbuf.at[s, pl.ds(2, rows)], own_sem)
@@ -65,44 +65,65 @@
         pltpu.make_async_copy(w3h.at[:, :, :, pl.ds(halves2[k], h2), :], w3.at[k], w_sem.at[5 + k])
         for k in range(2)
     ]
-    for load in load1 + load2 + load3:
+    load_b = [
+        pltpu.make_async_copy(src, dst, w_sem.at[7 + n])
+        for n, (src, dst) in enumerate(((b1h, b1), (b2h, b2), (b3h, b3)))
+    ]
+    for load in load_b + load1 + load2 + load3:
         load.start()
 
     barrier = pltpu.get_barrier_semaphore()
-    pl.semaphore_signal(barrier, inc=1, device_id=sib, device_id_type=MESH)
-
-    @pl.when(has_up)
-    def _():
-        pl.semaphore_signal(barrier, inc=1, device_id={"tile": up}, device_id_type=MESH)
-
-    @pl.when(has_down)
-    def _():
-        pl.semaphore_signal(barrier, inc=1, device_id={"tile": down}, device_id_type=MESH)
-
-    pl.semaphore_wait(barrier, 1 + has_up.astype(jnp.int32) + has_down.astype(jnp.int32))
+    even = lax.rem(t, 2) == 0
+    partner = jnp.where(even, t + 1, t - 1)
+    has_low, has_high = t >= 2, t + 2 < count
+    goes = jnp.where(even, has_high, has_low)
+    comes = jnp.where(even, has_low, has_high)
+    onward = lax.rem(jnp.where(even, t + 2, t + count - 2), count)
+    near_side = jnp.where(even, rows + 2, 0)
+    far_side = jnp.where(even, 0, rows + 2)
+
+    def greet(device):
+        pl.semaphore_signal(barrier, inc=1, device_id=device, device_id_type=MESH)
+
+    greet(sib)
+    greet({"tile": partner})
+    pl.when(has_low)(lambda: greet({"tile": lax.rem(t + count - 2, count)}))
+    pl.when(has_high)(lambda: greet({"tile": lax.rem(t + 2, count)}))
+    pl.semaphore_wait(barrier, 2 + has_low.astype(jnp.int32) + has_high.astype(jnp.int32))
 
     def remote(src, dst, send, recv, device):
         return pltpu.make_async_remote_copy(
             src_ref=src, dst_ref=dst, send_sem=send, recv_sem=recv, device_id=device, device_id_type=MESH
         )
 
-    plan = [
-        (rows - 1, 1, down, has_down, has_up),
-        (0, rows + 2, up, has_up, has_down),
-        (rows - 2, 0, down, has_down, has_up),
-        (1, rows + 3, up, has_up, has_down),
-    ]
-    direct = [
-        remote(feat.at[0, src], fbuf.at[s, dst], nb_send.at[n], nb_recv.at[n], {"tile": to})
-        for n, (src, dst, to, _, _) in enumerate(plan)
+    piece = cols // PIECES
+    chunks = [
+        (jnp.where(even, k, 1 - k), pl.ds(h * piece, piece)) for k in range(2) for h in range(PIECES)
+    ]
+    each = len(chunks)
+    theirs = [(1 - row, part) for row, part in chunks]
+    pair = [
+        remote(feat.at[0, row, part], fbuf.at[s, far_side + row, part], nb_send.at[n], nb_recv.at[n], {"tile": partner})
+        for n, (row, part) in enumerate(chunks)
+    ]
+    relay = [
+        remote(
+            fbuf.at[s, near_side + row, part], fbuf.at[s, far_side + row, part],
+            nb_send.at[each + n], nb_recv.at[each + n], {"tile": onward},
+        )
+        for n, (row, part) in enumerate(theirs)
     ]
     forward = [
-        remote(fbuf.at[s, dst], fbuf.at[s, dst], fw_send.at[n], fw_recv.at[n], sib)
-        for n, (_, dst, _, _, _) in enumerate(plan)
-    ]
-    swap = remote(feat.at[0], fbuf.at[s, pl.ds(2, rows)], fw_send.at[4], fw_recv.at[4], sib)
-    for n in range(4):
-        pl.when(plan[n][3])(direct[n].start)
+        remote(fbuf.at[s, side + row, part], fbuf.at[s, side + row, part], fw_send.at[n], fw_recv.at[n], sib)
+        for n, (side, row, part) in enumerate(
+            [(near_side, *c) for c in theirs] + [(far_side, *c) for c in theirs]
+        )
+    ]
+    swap = remote(
+        feat.at[0], fbuf.at[s, pl.ds(2, rows)], fw_send.at[2 * each], fw_recv.at[2 * each], sib
+    )
+    for c in pair:
+        c.start()
     swap.start()
 
     def silu_rows(frame, row, size):
@@ -110,41 +131,42 @@
             fbuf[frame, pl.ds(row, size)].astype(F32)
         ).astype(BF16).reshape(size * cols, c1)
 
-    for n in range(4):
-        dst = plan[n][1]
-
-        @pl.when(jnp.logical_not(plan[n][4]))
-        def _(dst=dst):
-            for f in range(2):
-                fbuf[f, dst] = jnp.zeros((cols, c1), BF16)
+    @pl.when(jnp.logical_not(comes))
+    def _():
+        for f in range(2):
+            for row in range(2):
+                fbuf[f, far_side + row] = jnp.zeros((cols, c1), BF16)
 
     def early1(j):
         load1[j].wait()
         for i in range(3):
             w1[0, i, j] = w1[0, i, j] + w1[1, i, j]
 
-    def pass_on(n):
-        @pl.when(plan[n][4])
+    def pass_pair(n):
+        pair[n].wait_recv()
+        pl.when(goes)(relay[n].start)
+        forward[n].start()
+
+    def pass_relay(first_one, stop):
+        @pl.when(comes)
         def _():
-            direct[n].wait_recv()
-            forward[n].start()
-
-    def arrived(n):
-        @pl.when(plan[n][4])
-        def _():
-            forward[n].wait_recv()
-        for f in range(2):
-            silu_rows(f, plan[n][1], 1)
-
+            for n in range(first_one, stop):
+                relay[n].wait_recv()
+                forward[each + n].start()
+
+    half = each // 2
+    for n in range(half):
+        pass_pair(n)
     early1(0)
+    for n in range(half, each):
+        pass_pair(n)
     early1(1)
     early1(2)
     own.wait()
     swap.wait_recv()
     for f in range(2):
         silu_rows(f, 2, rows)
-    pass_on(0)
-    pass_on(1)
+    pass_relay(0, half)
 
     def merge(buf, wide, half, c, size):
         def read(i, j):
@@ -179,9 +201,13 @@
 
         return later, sooner
 
-    bias1 = b1[:, pl.ds(o1, h1)].astype(F32)
-    bias2 = b2[:, pl.ds(o2, h2)].astype(F32)
-    bias3 = b3[...].astype(F32)
+    for load in load_b:
+        load.wait()
+    bias1 = b1[...].astype(F32).reshape(1, c1)
+    bias1 = jnp.where(s == 0, bias1[:, :h1], bias1[:, h1:])
+    bias2 = b2[...].astype(F32).reshape(1, c2)
+    bias2 = jnp.where(s == 0, bias2[:, :h2], bias2[:, h2:])
+    bias3 = b3[...].astype(F32).reshape(1, c3)
 
     def first(hidden_rows):
         def gather(frames):
@@ -230,8 +256,18 @@
                     mid[0, f, row] = value.astype(BF16)
                     at += cols
 
-    arrived(0)
-    arrived(1)
+    pass_relay(half, each)
+    for n in range(each):
+        forward[n].wait_recv()
+
+    @pl.when(comes)
+    def _():
+        for n in range(half):
+            forward[each + n].wait_recv()
+
+    for f in range(2):
+        silu_rows(f, 1, 1)
+        silu_rows(f, rows + 2, 1)
     first([(1, rows)])
     send_mid = [
         remote(mid.at[0, :, pl.ds(1, rows)], mid.at[1, :, pl.ds(1, rows)], mid_send.at[0], mid_recv.at[0], sib),
@@ -239,10 +275,15 @@
         remote(mid.at[0, :, rows + 1], mid.at[1, :, rows + 1], mid_send.at[2], mid_recv.at[2], sib),
     ]
     send_mid[0].start()
-    pass_on(2)
-    pass_on(3)
-    arrived(2)
-    arrived(3)
+
+    @pl.when(comes)
+    def _():
+        for n in range(half, each):
+            forward[each + n].wait_recv()
+
+    for f in range(2):
+        silu_rows(f, 0, 1)
+        silu_rows(f, rows + 3, 1)
     first([(0, 1), (rows + 1, 1)])
     send_mid[1].start()
     send_mid[2].start()
@@ -327,7 +368,6 @@
                 acc3[p, phase, outer] = value
     send_low[0].wait_recv()
     pl.when(s == 1)(send_low[1].wait_recv)
-    put = []
     for p in range(2):
         inner, outer = [], []
         for phase in range(2):
@@ -345,19 +385,18 @@
                 stage[p, m, pl.ds(n, cols, stride=4), :] = values[n][m * cols : (m + 1) * cols] + bias3
         for m in range(2 * rows):
             row = 2 * m + p
-            obuf[row] = stage[p, m].astype(BF16)
-    copy = pltpu.make_async_copy(obuf, out.at[0], out_sem)
-    copy.start()
-
-    for n in range(4):
-        pl.when(plan[n][3])(direct[n].wait_send)
-        pl.when(plan[n][4])(forward[n].wait_send)
+            out[0, row] = stage[p, m].astype(BF16)
+
+    for n in range(each):
+        pair[n].wait_send()
+        forward[n].wait_send()
+        pl.when(goes)(relay[n].wait_send)
+        pl.when(comes)(forward[each + n].wait_send)
     swap.wait_send()
     for c in send_mid:
         c.wait_send()
     send_low[0].wait_send()
     pl.when(s == 0)(send_low[1].wait_send)
-    copy.wait()
 
 
 def per_device(features, w1, b1, w2, b2, w3, b3):
@@ -365,17 +404,23 @@
     _, rows, cols, c1 = features.shape
     c2, c3 = w2.shape[4], w3.shape[4]
     h1, h2 = c1 // 2, c2 // 2
-    anywhere = pl.BlockSpec(memory_space=pl.ANY)
+    anywhere = pl.BlockSpec(memory_space=pltpu.HBM)
     vmem = pl.BlockSpec(memory_space=pltpu.VMEM)
     dma = pltpu.SemaphoreType.DMA
+    features, b1, b2, b3 = [
+        pltpu.with_memory_space_constraint(x, pltpu.HBM) for x in (features, b1, b2, b3)
+    ]
     return pl.pallas_call(
         functools.partial(kernel, count),
         out_shape=jax.ShapeDtypeStruct((1, 4 * rows, 4 * cols, c3), BF16),
-        in_specs=[anywhere, anywhere, vmem, anywhere, vmem, anywhere, vmem],
-        out_specs=anywhere,
+        in_specs=[anywhere] * 7,
+        out_specs=vmem,
         scratch_shapes=[
             pltpu.VMEM((2, rows + 4, cols, c1), BF16),
             pltpu.VMEM((2, (rows + 4) * cols, c1), BF16),
+            pltpu.VMEM((c1,), BF16),
+            pltpu.VMEM((c2,), BF16),
+            pltpu.VMEM((c3,), BF16),
             pltpu.VMEM((3, 3, 3, c1, h1), BF16),
             pltpu.VMEM((2, 3, 3, 3, h1, h2), BF16),
             pltpu.VMEM((2, 3, 3, 3, h2, c3), BF16),
@@ -386,14 +431,12 @@
             pltpu.VMEM((2, 2, 2, (rows + 1) * cols, 2 * h2), F32),
             pltpu.VMEM((2, 2, 2, 2 * rows * cols, 2 * c3), F32),
             pltpu.VMEM((2, 2 * rows, 4 * cols, c3), F32),
-            pltpu.VMEM((4 * rows, 4 * cols, c3), BF16),
-            dma((7,)),
+            dma((10,)),
             dma(()),
-            dma(()),
-            dma((4,)),
-            dma((4,)),
-            dma((5,)),
-            dma((5,)),
+            dma((4 * PIECES,)),
+            dma((4 * PIECES,)),
+            dma((4 * PIECES + 1,)),
+            dma((4 * PIECES + 1,)),
             dma((3,)),
             dma((3,)),
             dma((2,)),
@@ -402,7 +445,7 @@
         compiler_params=pltpu.CompilerParams(
             collective_id=0, has_side_effects=True, vmem_limit_bytes=52 * 2**20
         ),
-    )(features, w1, b1.reshape(1, c1), w2, b2.reshape(1, c2), w3, b3.reshape(1, c3))
+    )(features, w1, b1, w2, b2, w3, b3)
 
 
 def solution(mesh):

time: 21.9 us -> 18 us (0.82)
  local copies, waits for them, and re-layouts: 3.69 us -> 0.8 us
  Pallas kernels: 18 us -> 16.9 us
    unnamed x5 -> x1, local copies, waits for them, and re-layouts: 2.35 us -> 0.8 us
    reshape x2 -> x0, local copies, waits for them, and re-layouts: 1.34 us -> none  [the longest x1 0.68 us: per_device(): b1.reshape(1, c1)]
    pallas_call x1, Pallas kernels: 18 us -> 16.9 us  [per_device(): pl.pallas_call(functools.partial(kernel, count), out_shape=jax.ShapeDtype...]
where the time goes in v1:
time: 18 us; the launch traced here: 17.7 us
  Pallas kernels  16.9 us (94%)
  local copies, waits for them, and re-layouts  0.8 us (4%)
    pallas_call x1, Pallas kernels, per_device(): pl.pallas_call(functools.partial(kernel, count), out_shape=jax.ShapeDtype...  16.9 us
    unnamed x1, local copies, waits for them, and re-layouts  0.8 us

profile of v1, /device:TPU:9, one launch (start us, length us, event | category | flops | bytes accessed | tf_op | source)
XLA Modules:
  0.0 17.7 jit_solution(15632940411599193135)
XLA Ops:
  0.0 16.9 %shard_map.73 = bf16[1,8,256,128]{3,2,1,0:T(8,128)(2,1)S(1)} custom-call(bf16[1,2,64,512]{3,2,1,0:T(8,128)(2,1)} %feat.1, bf16[3,3,3,512,512]{4,3,2,1,0:T(8,128)(2,1)} %w1h.1, bf16[512]{0:T(512)(128)(2,1)} %b1h.1, bf16[3,3,3,512,256]{4,3,2,1,0:T(8,128)(2,1)} %w2h.1, bf16[256]{0:T(256)(128)(2,1)} %b2h.1, bf16[3,3,3,256,128]{4,3,2,1,0:T(8,128)(2,1)} %w3h.1, ...), custom_call_target="tpu_custom_call" | custom-call | tf_op jit(solution)/shard_map/pallas_call | solution.py:413
  16.9 0.8 %copy.9 = bf16[1,8,256,128]{3,2,1,0:T(8,128)(2,1)} copy(bf16[1,8,256,128]{3,2,1,0:T(8,128)(2,1)S(1)} %shard_map.73) | data formatting | bytes 1048576

commit v2 on v1

--- a/solution.py
+++ b/solution.py
@@ -69,7 +69,7 @@
         pltpu.make_async_copy(src, dst, w_sem.at[7 + n])
         for n, (src, dst) in enumerate(((b1h, b1), (b2h, b2), (b3h, b3)))
     ]
-    for load in load_b + load1 + load2 + load3:
+    for load in load_b + load1:
         load.start()
 
     barrier = pltpu.get_barrier_semaphore()
@@ -125,6 +125,8 @@
     for c in pair:
         c.start()
     swap.start()
+    for load in load2 + load3:
+        load.start()
 
     def silu_rows(frame, row, size):
         sbuf[frame, pl.ds(row * cols, size * cols), :] = silu(
@@ -268,13 +270,11 @@
     for f in range(2):
         silu_rows(f, 1, 1)
         silu_rows(f, rows + 2, 1)
-    first([(1, rows)])
     send_mid = [
         remote(mid.at[0, :, pl.ds(1, rows)], mid.at[1, :, pl.ds(1, rows)], mid_send.at[0], mid_recv.at[0], sib),
         remote(mid.at[0, :, 0], mid.at[1, :, 0], mid_send.at[1], mid_recv.at[1], sib),
         remote(mid.at[0, :, rows + 1], mid.at[1, :, rows + 1], mid_send.at[2], mid_recv.at[2], sib),
     ]
-    send_mid[0].start()
 
     @pl.when(comes)
     def _():
@@ -284,7 +284,8 @@
     for f in range(2):
         silu_rows(f, 0, 1)
         silu_rows(f, rows + 3, 1)
-    first([(0, 1), (rows + 1, 1)])
+    first([(0, rows + 2)])
+    send_mid[0].start()
     send_mid[1].start()
     send_mid[2].start()
 

time: 18 us -> 19.2 us (1.067)
  Pallas kernels: 16.9 us -> 18.2 us
    pallas_call x1, Pallas kernels: 16.9 us -> 18.2 us  [per_device(): pl.pallas_call(functools.partial(kernel, count), out_shape=jax.ShapeDtype...]
where the time goes in v2:
time: 19.2 us; the launch traced here: 19 us
  Pallas kernels  18.2 us (95%)
  local copies, waits for them, and re-layouts  0.8 us (4%)
    pallas_call x1, Pallas kernels, per_device(): pl.pallas_call(functools.partial(kernel, count), out_shape=jax.ShapeDtype...  18.2 us
    unnamed x1, local copies, waits for them, and re-layouts  0.8 us

profile of v2, /device:TPU:9, one launch (start us, length us, event | category | flops | bytes accessed | tf_op | source)
XLA Modules:
  0.0 19.0 jit_solution(15211228152697115589)
XLA Ops:
  0.0 18.2 %shard_map.73 = bf16[1,8,256,128]{3,2,1,0:T(8,128)(2,1)S(1)} custom-call(bf16[1,2,64,512]{3,2,1,0:T(8,128)(2,1)} %feat.1, bf16[3,3,3,512,512]{4,3,2,1,0:T(8,128)(2,1)} %w1h.1, bf16[512]{0:T(512)(128)(2,1)} %b1h.1, bf16[3,3,3,512,256]{4,3,2,1,0:T(8,128)(2,1)} %w2h.1, bf16[256]{0:T(256)(128)(2,1)} %b2h.1, bf16[3,3,3,256,128]{4,3,2,1,0:T(8,128)(2,1)} %w3h.1, ...), custom_call_target="tpu_custom_call" | custom-call | tf_op jit(solution)/shard_map/pallas_call | solution.py:414
  18.2 0.8 %copy.9 = bf16[1,8,256,128]{3,2,1,0:T(8,128)(2,1)} copy(bf16[1,8,256,128]{3,2,1,0:T(8,128)(2,1)S(1)} %shard_map.73) | data formatting | bytes 1048576
